TPU v7x, 32 devices: a whole 2x2x4 slice. The times are simulated.
32 devices in a mesh: narrow: 4 (over y, x), wide: 8 (over z, core).
Axes of the slice: x: 2, y: 2, z: 4, core: 2. Of those that a mesh axis runs over, the one named last changes fastest.
Arguments:
- tokens: bfloat16 [8, 2048, 768], P('wide', 'narrow'), may hold values from -6 to 6
- condition: bfloat16 [8, 2, 128], P('wide'), may hold values from -6 to 6
- docs_per_row: int32 [8], P('wide'), may hold values from 1 to 2, as said below
- w_ada: bfloat16 [128, 4608], replicated, may hold values from -0.5 to 0.5
- b_ada: bfloat16 [4608], replicated, may hold values from -3 to 3
- gain_one: bfloat16 [768], replicated, may hold values from 0.25 to 1.75
- w_qkv: bfloat16 [768, 2304], replicated, may hold values from -0.21875 to 0.21875
- w_out: bfloat16 [768, 768], replicated, may hold values from -1.75 to 1.75
- gain_two: bfloat16 [768], replicated, may hold values from 0.25 to 1.75
- w_up: bfloat16 [768, 3072], replicated, may hold values from -0.21875 to 0.21875
- b_up: bfloat16 [3072], replicated, may hold values from -3 to 3
- w_down: bfloat16 [3072, 768], replicated, may hold values from -0.109375 to 0.109375
- b_down: bfloat16 [768], replicated, may hold values from -3 to 3
- cotangent: bfloat16 [8, 2048, 768], P('wide', 'narrow'), may hold values from -6 to 6
Outputs:
- output: bfloat16 [8, 2048, 768], P('wide', 'narrow')
- grad_tokens: float32 [8, 2048, 768], P('wide', 'narrow')
- grad_condition: float32 [8, 2, 128], P('wide')
- grad_w_ada: float32 [128, 4608], P(None, 'wide')
- grad_b_ada: float32 [4608], P('wide')
- grad_gain_one: float32 [768], P('wide')
- grad_w_qkv: float32 [768, 2304], P('wide')
- grad_w_out: float32 [768, 768], P('wide')
- grad_gain_two: float32 [768], P('wide')
- grad_w_up: float32 [768, 3072], P('wide')
- grad_b_up: float32 [3072], P('wide')
- grad_w_down: float32 [3072, 768], P('wide')
- grad_b_down: float32 [768], P('wide')
Inputs may be any that keep to these rules, and one draw needn't show every extreme that they name: `docs_per_row`: each entry is 1 (the row is one sequence of 2048 tokens) or 2 (the row holds 2 sequences of 1024 tokens). In every draw the rows of some index of wide are all of the first kind and those of another index all of the second.
All inputs are finite; a program needn't handle non-finite values.
Results may differ from a plain program's by a relative error of at most 0.014.
The roundings to bfloat16 on the way count: a program that leaves them out, or rounds other values in their place, can miss the bound.
Values may be sent and summed in bfloat16 or wider, within the bound.
A program may use at most 192 MiB of HBM per device.

v0:
```python
import jax
import jax.numpy as jnp
from jax import lax
from jax.sharding import PartitionSpec as P

HEADS = 12
HEAD_DIM = 64
DOCS = 2
EPS = 1e-05
HIGH = lax.Precision.HIGHEST


def normalize(values):
    mean = jnp.mean(values, axis=-1, keepdims=True)
    centred = values - mean
    spread = jnp.mean(centred * centred, axis=-1, keepdims=True)
    return centred * lax.rsqrt(spread + EPS)


def modulated(values, gain, shift, scale):
    return normalize(values) * gain * (1.0 + scale) + shift


def gelu_tanh(values):
    return (
        0.5
        * values
        * (1.0 + jnp.tanh(0.7978845608028654 * (values + 0.044715 * values * values * values)))
    )


def rotate(values, cosine, sine):
    half = values.shape[-1] // 2
    turned = jnp.concatenate([-values[..., half:], values[..., :half]], axis=-1)
    return values * cosine + turned * sine


def angles(position, head_dim):
    freq = 10000.0 ** (-jnp.arange(head_dim // 2, dtype=jnp.float32) * 2.0 / head_dim)
    angle = position.astype(jnp.float32)[..., None] * freq
    angle = jnp.concatenate([angle, angle], axis=-1)
    return (jnp.cos(angle), jnp.sin(angle))


def attend(query, keys, values, docs):
    length, group, head_dim = query.shape
    count = length // docs
    block = min(512, count)
    factor = head_dim ** (-0.5)
    keys_doc = keys.reshape(count, docs, group, head_dim)
    values_doc = values.reshape(count, docs, group, head_dim)
    pieces = query.reshape(count // block, block, docs, group, head_dim)

    def one_block(piece):
        scores = (
            jnp.einsum("qshd,kshd->shqk", piece, keys_doc, preferred_element_type=jnp.float32)
            * factor
        )
        top = jnp.max(scores, axis=-1, keepdims=True)
        weights = jnp.exp(scores - top)
        total = jnp.sum(weights, axis=-1, keepdims=True)
        probs = (weights / total).astype(jnp.bfloat16)
        mixed = jnp.einsum("shqk,kshd->qshd", probs, values_doc, preferred_element_type=jnp.float32)
        return (mixed.astype(jnp.bfloat16), (top + jnp.log(total))[..., 0])

    mixed, logsum = lax.map(one_block, pieces)
    logsum = jnp.transpose(logsum, (0, 3, 1, 2)).reshape(length, group)
    return (mixed.reshape(length, group, head_dim), logsum)


def attend_back(query, keys, values, logsum, grad_out, docs):
    length, group, head_dim = query.shape
    count = length // docs
    block = min(512, count)
    factor = head_dim ** (-0.5)
    keys_doc = keys.reshape(count, docs, group, head_dim)
    values_doc = values.reshape(count, docs, group, head_dim)
    pieces = query.reshape(count // block, block, docs, group, head_dim)
    sum_pieces = logsum.reshape(count // block, block, docs, group)
    grad_pieces = grad_out.reshape(count // block, block, docs, group, head_dim)

    def step(carry, item):
        grad_keys, grad_values = carry
        piece, sum_piece, grad_piece = item
        scores = (
            jnp.einsum("qshd,kshd->shqk", piece, keys_doc, preferred_element_type=jnp.float32)
            * factor
        )
        probs = jnp.exp(scores - jnp.transpose(sum_piece, (1, 2, 0))[..., None])
        low_probs = probs.astype(jnp.bfloat16)
        grad_values = grad_values + jnp.einsum(
            "shqk,qshd->kshd", low_probs, grad_piece, preferred_element_type=jnp.float32
        )
        grad_probs = jnp.einsum(
            "qshd,kshd->shqk", grad_piece, values_doc, preferred_element_type=jnp.float32
        )
        centre = jnp.sum(grad_probs * probs, axis=-1, keepdims=True)
        grad_scores = (probs * (grad_probs - centre)).astype(jnp.bfloat16)
        grad_query = (
            jnp.einsum("shqk,kshd->qshd", grad_scores, keys_doc, preferred_element_type=jnp.float32)
            * factor
        )
        grad_keys = (
            grad_keys
            + jnp.einsum("shqk,qshd->kshd", grad_scores, piece, preferred_element_type=jnp.float32)
            * factor
        )
        return ((grad_keys, grad_values), grad_query)

    zeros = jnp.zeros((count, docs, group, head_dim), jnp.float32)
    (grad_keys, grad_values), grad_query = lax.scan(
        step, (zeros, zeros), (pieces, sum_pieces, grad_pieces)
    )
    shape = (length, group, head_dim)
    return (
        grad_query.reshape(shape).astype(jnp.bfloat16),
        grad_keys.reshape(shape).astype(jnp.bfloat16),
        grad_values.reshape(shape).astype(jnp.bfloat16),
    )


def attend_row(item):
    query, keys, values, docs = item
    return lax.cond(
        docs == 1, lambda: attend(query, keys, values, 1), lambda: attend(query, keys, values, DOCS)
    )


def back_row(item):
    query, keys, values, logsum, grad_out, docs = item
    return lax.cond(
        docs == 1,
        lambda: attend_back(query, keys, values, logsum, grad_out, 1),
        lambda: attend_back(query, keys, values, logsum, grad_out, DOCS),
    )


def body(
    tokens,
    condition,
    docs_per_row,
    w_ada,
    b_ada,
    gain_one,
    w_qkv,
    w_out,
    gain_two,
    w_up,
    b_up,
    w_down,
    b_down,
    cotangent,
):
    count_rows, local, width = tokens.shape
    shards = lax.axis_size("narrow")
    group = HEADS // shards
    head_dim = HEAD_DIM
    length = local * shards
    index = lax.axis_index("narrow") * local + jnp.arange(local, dtype=jnp.int32)
    kinds = docs_per_row[:, None]
    segment = index[None, :] % kinds
    position = index[None, :] // kinds
    cosine, sine = angles(position, head_dim)
    cosine = cosine[:, :, None, :]
    sine = sine[:, :, None, :]
    onehot = (segment[:, :, None] == jnp.arange(DOCS, dtype=jnp.int32)).astype(jnp.float32)
    mods = jnp.einsum(
        "rsc,cm->rsm", condition, w_ada, preferred_element_type=jnp.float32
    ) + b_ada.astype(jnp.float32)
    per_token = jnp.einsum("rls,rsm->rlm", onehot, mods, precision=HIGH)
    shift_one, scale_one, gate_one, shift_two, scale_two, gate_two = jnp.split(
        per_token, 6, axis=-1
    )
    inputs = tokens.astype(jnp.float32)
    first_in, first_back = jax.vjp(
        modulated, inputs, gain_one.astype(jnp.float32), shift_one, scale_one
    )
    first_low = first_in.astype(jnp.bfloat16).reshape(-1, width)
    projected = jnp.dot(first_low, w_qkv, preferred_element_type=jnp.float32).reshape(
        count_rows, local, 3, HEADS, head_dim
    )
    query_rot, turn_back = jax.vjp(lambda values: rotate(values, cosine, sine), projected[:, :, 0])
    key_rot = rotate(projected[:, :, 1], cosine, sine)

    def to_heads(values):
        return values.astype(jnp.bfloat16).reshape(count_rows, local, shards, group * head_dim)

    def head_view(values):
        return values.reshape(count_rows, length, group, head_dim)

    query_h, key_h, value_h = (
        lax.all_to_all(to_heads(query_rot), "narrow", split_axis=2, concat_axis=1, tiled=True),
        lax.all_to_all(to_heads(key_rot), "narrow", split_axis=2, concat_axis=1, tiled=True),
        lax.all_to_all(
            to_heads(projected[:, :, 2]), "narrow", split_axis=2, concat_axis=1, tiled=True
        ),
    )
    query_h = head_view(query_h)
    key_h = head_view(key_h)
    value_h = head_view(value_h)
    mixed_h, logsum = lax.map(attend_row, (query_h, key_h, value_h, docs_per_row))
    mixed = lax.all_to_all(
        mixed_h.reshape(count_rows, length, 1, group * head_dim),
        "narrow",
        split_axis=1,
        concat_axis=2,
        tiled=True,
    )
    attended = mixed.reshape(count_rows * local, width)
    branch = jnp.dot(attended, w_out, preferred_element_type=jnp.float32).reshape(
        count_rows, local, width
    )
    middle = inputs + gate_one * branch
    second_in, second_back = jax.vjp(
        modulated, middle, gain_two.astype(jnp.float32), shift_two, scale_two
    )
    second_low = second_in.astype(jnp.bfloat16).reshape(-1, width)
    hidden = jnp.dot(second_low, w_up, preferred_element_type=jnp.float32) + b_up.astype(
        jnp.float32
    )
    active, active_back = jax.vjp(gelu_tanh, hidden)
    active_low = active.astype(jnp.bfloat16)
    down = (
        jnp.dot(active_low, w_down, preferred_element_type=jnp.float32) + b_down.astype(jnp.float32)
    ).reshape(count_rows, local, width)
    output = (middle + gate_two * down).astype(jnp.bfloat16)
    grad_y = cotangent.astype(jnp.float32)
    grad_gate_two = grad_y * down
    grad_down = (grad_y * gate_two).astype(jnp.bfloat16).reshape(-1, width)
    sum_b_down = jnp.sum(grad_down.astype(jnp.float32), axis=0)
    sum_w_down = jnp.einsum("tf,td->fd", active_low, grad_down, preferred_element_type=jnp.float32)
    grad_active = jnp.einsum("td,fd->tf", grad_down, w_down, preferred_element_type=jnp.float32)
    grad_hidden = active_back(grad_active)[0].astype(jnp.bfloat16)
    sum_b_up = jnp.sum(grad_hidden.astype(jnp.float32), axis=0)
    sum_w_up = jnp.einsum("td,tf->df", second_low, grad_hidden, preferred_element_type=jnp.float32)
    grad_second = jnp.einsum(
        "tf,df->td", grad_hidden, w_up, preferred_element_type=jnp.float32
    ).reshape(count_rows, local, width)
    grad_middle_norm, sum_gain_two, grad_shift_two, grad_scale_two = second_back(grad_second)
    grad_middle = grad_y + grad_middle_norm
    grad_gate_one = grad_middle * branch
    grad_branch = (grad_middle * gate_one).astype(jnp.bfloat16).reshape(-1, width)
    sum_w_out = jnp.einsum("td,te->de", attended, grad_branch, preferred_element_type=jnp.float32)
    grad_attended = jnp.einsum(
        "te,de->td", grad_branch, w_out, preferred_element_type=jnp.float32
    ).astype(jnp.bfloat16)
    grad_mixed = lax.all_to_all(
        grad_attended.reshape(count_rows, local, shards, group * head_dim),
        "narrow",
        split_axis=2,
        concat_axis=1,
        tiled=True,
    )
    grad_mixed = head_view(grad_mixed)
    grad_query_h, grad_key_h, grad_value_h = lax.map(
        back_row, (query_h, key_h, value_h, logsum, grad_mixed, docs_per_row)
    )

    def from_heads(values):
        return values.reshape(count_rows, length, 1, group * head_dim)

    grad_query, grad_key, grad_value = (
        lax.all_to_all(from_heads(grad_query_h), "narrow", split_axis=1, concat_axis=2, tiled=True),
        lax.all_to_all(from_heads(grad_key_h), "narrow", split_axis=1, concat_axis=2, tiled=True),
        lax.all_to_all(from_heads(grad_value_h), "narrow", split_axis=1, concat_axis=2, tiled=True),
    )
    seq_shape = (count_rows, local, HEADS, head_dim)
    grad_query_raw = turn_back(grad_query.reshape(seq_shape).astype(jnp.float32))[0]
    grad_key_raw = turn_back(grad_key.reshape(seq_shape).astype(jnp.float32))[0]
    grad_projected = jnp.stack(
        [grad_query_raw, grad_key_raw, grad_value.reshape(seq_shape).astype(jnp.float32)], axis=2
    )
    grad_projected = grad_projected.astype(jnp.bfloat16).reshape(-1, 3 * width)
    sum_w_qkv = jnp.einsum(
        "td,te->de", first_low, grad_projected, preferred_element_type=jnp.float32
    )
    grad_first = jnp.einsum(
        "te,de->td", grad_projected, w_qkv, preferred_element_type=jnp.float32
    ).reshape(count_rows, local, width)
    grad_inputs_norm, sum_gain_one, grad_shift_one, grad_scale_one = first_back(grad_first)
    grad_inputs = grad_middle + grad_inputs_norm
    grad_per = jnp.concatenate(
        [
            grad_shift_one,
            grad_scale_one,
            grad_gate_one,
            grad_shift_two,
            grad_scale_two,
            grad_gate_two,
        ],
        axis=-1,
    )
    grad_mods = jnp.einsum("rls,rlm->rsm", onehot, grad_per, precision=HIGH)
    sum_b_ada = jnp.sum(grad_mods, axis=(0, 1))
    sum_w_ada_turned = jnp.einsum(
        "rsm,rsc->mc", grad_mods, condition.astype(jnp.float32), precision=HIGH
    )
    grad_cond_part = jnp.einsum("rsm,cm->rsc", grad_mods, w_ada.astype(jnp.float32), precision=HIGH)
    (
        share_ada,
        share_qkv,
        share_out,
        share_up,
        share_down,
        piece_ada,
        piece_one,
        piece_two,
        piece_up,
        piece_down,
    ) = (
        lax.psum_scatter(sum_w_ada_turned, "wide", scatter_dimension=0, tiled=True),
        lax.psum_scatter(sum_w_qkv, "wide", scatter_dimension=0, tiled=True),
        lax.psum_scatter(sum_w_out, "wide", scatter_dimension=0, tiled=True),
        lax.psum_scatter(sum_w_up, "wide", scatter_dimension=0, tiled=True),
        lax.psum_scatter(sum_w_down, "wide", scatter_dimension=0, tiled=True),
        lax.psum_scatter(sum_b_ada, "wide", scatter_dimension=0, tiled=True),
        lax.psum_scatter(sum_gain_one, "wide", scatter_dimension=0, tiled=True),
        lax.psum_scatter(sum_gain_two, "wide", scatter_dimension=0, tiled=True),
        lax.psum_scatter(sum_b_up, "wide", scatter_dimension=0, tiled=True),
        lax.psum_scatter(sum_b_down, "wide", scatter_dimension=0, tiled=True),
    )
    (
        total_ada,
        total_qkv,
        total_out,
        total_up,
        total_down,
        vector_ada,
        vector_one,
        vector_two,
        vector_up,
        vector_down,
        grad_condition,
    ) = lax.psum(
        (
            share_ada,
            share_qkv,
            share_out,
            share_up,
            share_down,
            piece_ada,
            piece_one,
            piece_two,
            piece_up,
            piece_down,
            grad_cond_part,
        ),
        "narrow",
    )
    return (
        output,
        grad_inputs,
        grad_condition,
        total_ada.T,
        vector_ada,
        vector_one,
        total_qkv,
        total_out,
        vector_two,
        total_up,
        vector_up,
        total_down,
        vector_down,
    )


def solution(mesh):
    in_specs = (
        P("wide", "narrow", None),
        P("wide", None, None),
        P("wide"),
        P(),
        P(),
        P(),
        P(),
        P(),
        P(),
        P(),
        P(),
        P(),
        P(),
        P("wide", "narrow", None),
    )
    out_specs = (
        P("wide", "narrow", None),
        P("wide", "narrow", None),
        P("wide", None, None),
        P(None, "wide"),
        P("wide"),
        P("wide"),
        P("wide", None),
        P("wide", None),
        P("wide"),
        P("wide", None),
        P("wide"),
        P("wide", None),
        P("wide"),
    )
    return jax.shard_map(body, mesh=mesh, in_specs=in_specs, out_specs=out_specs, check_vma=False)
```

profile of v0, /device:TPU:0, one launch (start us, length us, event | category | flops | bytes accessed | tf_op | source)
XLA Modules:
  0.0 913.8 jit_solution(2107163655373730929)
XLA Ops:
  12.2 5.9 copy.309
  19.0 3.9 convolution_bitcast_fusion
  23.5 4.2 copy-done.38
  32.1 5.2 all-to-all-start.2
  43.5 4.6 all-to-all-done.2
  48.1 13.2 %all_to_all.102 = bf16[1,512,4,192]{1,3,0,2:T(8,128)(2,1)S(1)} all-to-all(bf16[1,512,4,192]{1,3,0,2:T(8,128)(2,1)S(1)} %get-tuple-element.723), channel_id=1, replica_groups=mesh['narrow'=4,'wide'=8] {'narrow'}, dimensions={2} | all-to-all | bytes 1572864 | tf_op jit(solution)/shard_map/all_to_all | solution.py:193
  78.2 46.7 %conditional.2 = (bf16[2048,3,64]{2,1,0:T(4,128)(2,1)}, f32[2048,3]{1,0:T(8,128)}) conditional(s32[]{:T(128)} %convert_element_type.263, (bf16[2048,3,64]{0,2,1:T(8,128)(2,1)}, bf16[2048,3,64]{0,2,1:T(8,128)(2,1)S(1)}, bf16[2048,3,64]{0,2,1:T(8,128)(2,1)S(1)}) %tuple.47, (bf16[2048,3,64]{0,2,1:T(8,128)(2,1)}, bf16[2048,3,64]{0,2,1:T(8,128)(2,1)S(1)}, ...), branch_computations={%region_2.7_spmd, %region_7.12_spmd} | conditional | flops 833811456 | bytes 60920124 | solution.py:124
  82.7 36.1 %while.50 = (s32[]{:T(128)}, bf16[4,512,1,3,64]{1,4,3,2,0:T(8,128)(2,1)}, f32[4,1,3,512]{3,2,1,0:T(4,128)}, bf16[4,512,1,3,64]{1,4,3,2,0:T(8,128)(2,1)S(1)}, bf1...) while((s32[]{:T(128)}, bf16[4,512,1,3,64]{1,4,3,2,0:T(8,128)(2,1)}, ...), condition=%wide.region_11.11_spmd, body=%wide.region_8.10_spmd.sunk | while | flops 833714688 | bytes 39766112 | solution.py:66
  87.1 4.0 fusion.244
  96.1 4.0 fusion.244
  105.1 4.0 fusion.244
  114.1 4.0 fusion.244
  120.8 4.0 copy.294
  127.7 3.8 copy.320
  132.0 13.6 %reduce.17 = bf16[2048,192]{1,0:T(8,128)(2,1)} reduce(bf16[2048,1,1,192]{3,2,1,0:T(2,128)(2,1)} %bitcast.455, bf16[]{:T(256)} %broadcast.557), dimensions={1,2}, to_apply=%bitcast.292.reduce_sub_computation | reduce | bytes 1572866
  145.6 4.0 reshape.986
  149.6 4.7 all-to-all-start.3
  158.7 4.1 all-to-all-done.3
  162.8 4.2 reshape.987
  166.9 5.7 copy.321
  177.2 3.8 fusion.147
  186.6 11.7 %convert_reduce_fusion = (f32[3072]{0:T(1024)}, bf16[512,3072]{1,0:T(8,128)(2,1)S(1)}) fusion(f32[512,3072]{1,0:T(8,128)S(1)} %fusion.152, f32[3072]{0:T(1024)S(1)} %copy-done.87, bf16[512,768]{1,0:T(8,128)(2,1)S(1)} %copy-done.53, bf16[3072,768]{1,0:T(8,128)(2,1)} %param.37), kind=kOutput, calls=%fused_computation.105 | convolution fusion | flops 2458383360 | bytes 14966784 | tf_op jit(solution)/shard_map/td,fd->tf/dot_general | solution.py:232
  202.1 8.5 fusion.146
  215.8 11.2 %all_to_all.103 = bf16[1,512,4,192]{1,3,0,2:T(8,128)(2,1)S(1)} all-to-all(bf16[1,512,4,192]{1,3,0,2:T(8,128)(2,1)S(1)} %bitcast.488), channel_id=1, replica_groups=mesh['narrow'=4,'wide'=8] {'narrow'}, dimensions={2} | all-to-all | bytes 1572864 | tf_op jit(solution)/shard_map/all_to_all | solution.py:247
  229.1 117.1 %conditional.3 = (bf16[2048,3,64]{2,1,0:T(4,128)(2,1)}, bf16[2048,3,64]{2,1,0:T(4,128)(2,1)}, bf16[2048,3,64]{2,1,0:T(4,128)(2,1)S(1)}) conditional(s32[]{:T(128)} %convert_element_type.263, (bf16[2048,3,64]{0,2,1:T(8,128)(2,1)}, f32[2048,3]{1,0:T(8,128)S(1)}, bf16[2048,3,64]{0,2,1:T(8,128)(2,1)}, bf16[2048,3,64]{0,2,1:T(8,128)(2,1)S(1)}, ...), branch_computations={%region_16.20_spmd, %region_20.24_spmd} | conditional | flops 2053174272 | bytes 155857408 | solution.py:131
  239.2 96.6 %while.53 = (s32[]{:T(128)}, f32[2048,1,3,64]{0,3,2,1:T(8,128)}, f32[2048,1,3,64]{0,3,2,1:T(8,128)}, bf16[4,512,1,3,64]{1,4,3,2,0:T(8,128)(2,1)}, bf16[4,512,1,3...) while((s32[]{:T(128)}, f32[2048,1,3,64]{0,3,2,1:T(8,128)}, ...), condition=%wide.region_23.23_spmd.clone, body=%wide.region_21.22_spmd.clone.sunk | while | flops 2053077504 | bytes 129415344 | solution.py:111
  248.4 4.7 multiply_convert_fusion.8
  253.1 5.6 fusion.230
  263.1 5.1 fusion.229
  271.8 4.7 multiply_convert_fusion.8
  276.5 5.6 fusion.230
  282.2 3.9 fusion.228
  287.9 5.1 fusion.229
  296.6 4.7 multiply_convert_fusion.8
  301.3 5.6 fusion.230
  307.0 3.9 fusion.228
  312.7 5.1 fusion.229
  321.5 4.7 multiply_convert_fusion.8
  326.2 5.6 fusion.230
  331.8 3.9 fusion.228
  335.7 4.2 copy.306
  349.1 3.8 copy.337
  352.9 12.7 %reduce.20 = bf16[2048,192]{1,0:T(8,128)(2,1)S(1)} reduce(bf16[2048,1,1,192]{3,2,1,0:T(2,128)(2,1)} %bitcast.458, bf16[]{:T(256)} %broadcast.557), dimensions={1,2}, to_apply=%bitcast.296.reduce_sub_computation | reduce | bytes 1572866
  367.9 4.2 all-to-all-start.6
  375.0 3.8 copy.333
  378.7 13.6 %reduce.19 = bf16[2048,192]{1,0:T(8,128)(2,1)} reduce(bf16[2048,1,1,192]{3,2,1,0:T(2,128)(2,1)} %bitcast.459, bf16[]{:T(256)} %broadcast.557), dimensions={1,2}, to_apply=%bitcast.298.reduce_sub_computation | reduce | bytes 1572866
  392.4 4.0 reshape.992
  396.4 4.2 all-to-all-start.5
  407.0 11.6 %reduce.18 = bf16[2048,192]{1,0:T(8,128)(2,1)S(1)} reduce(bf16[2048,1,1,192]{3,2,1,0:T(2,128)(2,1)S(1)} %bitcast.456, bf16[]{:T(256)} %broadcast.557), dimensions={1,2}, to_apply=%bitcast.294.reduce_sub_computation | reduce | bytes 1572866
  429.3 4.1 all-to-all-start.7
  433.5 4.2 reshape.993
  437.7 4.5 copy.334
  452.1 4.9 copy.342
  473.9 3.8 fusion.151
  481.3 5.0 fusion.120
  487.4 10.4 %fusion.142 = f32[3072,768]{1,0:T(8,128)} fusion(bf16[512,768]{1,0:T(8,128)(2,1)S(1)} %copy-done.54, f32[512,3072]{1,0:T(8,128)} %copy-done.28, f32[3072]{0:T(1024)S(1)} %copy-done.88), kind=kOutput, calls=%fused_computation.224 | convolution fusion | flops 2431647744 | bytes 16527360 | tf_op jit(solution)/shard_map/tf,td->fd/dot_general | solution.py:231
  499.0 7.0 fusion.154
  506.2 13.5 %reduce-scatter.6.cloned.1.call-done = f32[576,128]{1,0:T(8,128)} async-done(((f32[4608,128]{1,0:T(8,128)}), f32[576,128]{1,0:T(8,128)}) %reduce-scatter.6.cloned.1.call-update) | async-done | bytes 294928 | tf_op jit(solution)/shard_map/reduce_scatter | solution.py:311
  519.6 78.7 %reduce-scatter.8.cloned.1.call-done = f32[96,2304]{1,0:T(8,128)} async-done(((f32[768,2304]{1,0:T(8,128)}), f32[96,2304]{1,0:T(8,128)}) %reduce-scatter.8.cloned.1.call-update) | async-done | bytes 884752 | tf_op jit(solution)/shard_map/reduce_scatter | solution.py:312
  598.3 100.1 %reduce-scatter.14.cloned.1.call-done = f32[384,768]{1,0:T(8,128)} async-done(((f32[3072,768]{1,0:T(8,128)}), f32[384,768]{1,0:T(8,128)}) %reduce-scatter.14.cloned.1.call-update) | async-done | bytes 1179664 | tf_op jit(solution)/shard_map/reduce_scatter | solution.py:315
  698.4 100.0 %reduce-scatter.12.cloned.1.call-done = f32[96,3072]{1,0:T(8,128)} async-done(((f32[768,3072]{1,0:T(8,128)}), f32[96,3072]{1,0:T(8,128)}) %reduce-scatter.12.cloned.1.call-update) | async-done | bytes 1179664 | tf_op jit(solution)/shard_map/reduce_scatter | solution.py:314
  801.1 26.4 %all-reduce.9 = (f32[4608]{0:T(1024)S(1)}, f32[768]{0:T(1024)S(1)}, f32[768]{0:T(1024)S(1)}, f32[3072]{0:T(1024)S(1)}, f32[768]{0:T(1024)S(1)}) all-reduce(f32[4608]{0:T(1024)S(1)} %copy-done.65, f32[768]{0:T(1024)S(1)} %get-tuple-element.622, f32[768]{0:T(1024)S(1)} %copy-done.91, ...), channel_id=3, replica_groups=mesh['narrow'=4,'wide'=8] {'wide'}, use_global_device_ids=true, to_apply=%region_30.31.clone | all-reduce | flops 9984 | bytes 79872
  828.9 10.9 %all-reduce.10 = (f32[1,2,128]{2,1,0:T(2,128)}, f32[576]{0:T(1024)}, f32[96]{0:T(128)}, f32[96]{0:T(128)}, f32[384]{0:T(512)}, /*index=5*/f32[96]{0:T(128)}) all-reduce(f32[1,2,128]{2,1,0:T(2,128)S(1)} %convolution_bitcast_fusion.2, f32[576]{0:T(1024)S(1)} %dynamic-slice.2, ...), channel_id=1, replica_groups=mesh['narrow'=4,'wide'=8] {'narrow'}, use_global_device_ids=true, to_apply=%region_26.27 | all-reduce | flops 1504 | bytes 12032 | tf_op jit(solution)/shard_map/psum | solution.py:334
  839.7 60.2 %all-reduce.14.cloned.1.call-done = (f32[128,576]{0,1:T(8,128)}, f32[96,2304]{1,0:T(8,128)}, f32[96,768]{1,0:T(8,128)}, f32[96,3072]{1,0:T(8,128)}, f32[384,768]{1,0:T(8,128)}) async-done(((f32[128,576]{0,1:T(8,128)}, f32[96,2304]{1,0:T(8,128)}, f32[96,768]{1,0:T(8,128)}, f32[96,3072]{1,0:T(8,128)}, f32[384,768]{1,0:T(8,128)}), (f32[128,576]{0,1:T(8,128)}, f32[96,2304]{1,0:T(8,128)}, f32[96,768]{1,0:T(8,128)}, ...) | async-done | bytes 3833872 | tf_op jit(solution)/shard_map/psum | solution.py:334
  (334 shorter events, 198.0 us)
Async XLA Ops:
  7.2 170.0 %copy-start = (bf16[768,768]{1,0:T(8,128)(2,1)S(1)}, bf16[768,768]{1,0:T(8,128)(2,1)}, u32[]{:S(2)}) copy-start(bf16[768,768]{1,0:T(8,128)(2,1)} %param.33) | copy-start | bytes 3538948
  9.3 13.7 %copy-start.68 = (f32[512]{0:T(512)}, f32[512]{0:T(512)S(1)}, u32[]{:S(2)}) copy-start(f32[512]{0:T(512)S(1)} %broadcast_multiply_fusion.4) | copy-start | bytes 6148
  10.8 12.2 %copy-start.70 = (f32[512]{0:T(512)}, f32[512]{0:T(512)S(1)}, u32[]{:S(2)}) copy-start(f32[512]{0:T(512)S(1)} %fusion.136) | copy-start | bytes 6148
  11.5 11.5 %copy-start.63 = (f32[768]{0:T(1024)}, f32[768]{0:T(1024)S(1)}, u32[]{:S(2)}) copy-start(f32[768]{0:T(1024)S(1)} %convert_element_type.264) | copy-start | bytes 9220
  12.2 5.9 copy-start.35
  12.2 5.9 copy-start.93
  19.0 3.9 copy-start.7
  23.0 6.7 copy-start.6
  23.0 4.7 copy-start.38
  23.5 6.2 copy-start.40
  32.1 16.0 %all-to-all-start.2 = ((bf16[1,512,4,192]{1,3,0,2:T(8,128)(2,1)}), bf16[1,512,4,192]{1,3,0,2:T(8,128)(2,1)S(1)}, u32[]{:S(2)}, u32[]{:S(2)}) async-start(bf16[1,512,4,192]{1,3,0,2:T(8,128)(2,1)} %bitcast.65), calls=%async_computation.2 | async-start | bytes 1572864 | tf_op jit(solution)/shard_map/all_to_all | solution.py:194
  61.3 12.6 %all-to-all-start = ((bf16[1,512,4,192]{1,3,0,2:T(8,128)(2,1)}), bf16[1,512,4,192]{1,3,0,2:T(8,128)(2,1)S(1)}, u32[]{:S(2)}, u32[]{:S(2)}) async-start(bf16[1,512,4,192]{1,3,0,2:T(8,128)(2,1)} %get-tuple-element.724), calls=%async_computation | async-start | bytes 1572864 | tf_op jit(solution)/shard_map/all_to_all | solution.py:192
  145.6 8.7 copy-start.92
  145.6 9.4 %copy-start.90 = (bf16[3072]{0:T(1024)(128)(2,1)S(1)}, bf16[3072]{0:T(1024)(128)(2,1)}, u32[]{:S(2)}) copy-start(bf16[3072]{0:T(1024)(128)(2,1)} %param.36) | copy-start | bytes 18436
  145.6 10.0 %copy-start.18 = (bf16[1,512,768]{2,1,0:T(8,128)(2,1)S(1)}, bf16[1,512,768]{2,1,0:T(8,128)(2,1)}, u32[]{:S(2)}) copy-start(bf16[1,512,768]{2,1,0:T(8,128)(2,1)} %param.39) | copy-start | bytes 2359300
  149.6 13.1 %all-to-all-start.3 = ((bf16[4,2,49152]{2,1,0:T(2,128)(2,1)}), bf16[4,2,49152]{2,1,0:T(2,128)(2,1)}, u32[]{:S(2)}, u32[]{:S(2)}) async-start(bf16[4,2,49152]{2,1,0:T(2,128)(2,1)} %reshape.986), calls=%async_computation.3 | async-start | bytes 1572864 | tf_op jit(solution)/shard_map/all_to_all | solution.py:202
  154.3 47.7 %copy-start.72 = (f32[768]{0:T(1024)}, f32[768]{0:T(1024)S(1)}, u32[]{:S(2)}) copy-start(f32[768]{0:T(1024)S(1)} %convert_element_type.270) | copy-start | bytes 9220
  155.0 47.0 %copy-start.84 = (f32[768]{0:T(1024)}, f32[768]{0:T(1024)S(1)}, u32[]{:S(2)}) copy-start(f32[768]{0:T(1024)S(1)} %convert_element_type.274) | copy-start | bytes 9220
  172.7 4.5 copy-start.8
  175.7 8.2 slice-start.3
  177.1 3.8 copy-start.26
  177.2 6.7 slice-start.4
  181.0 21.1 %copy-start.12 = (f32[1,512,768]{2,1,0:T(8,128)}, f32[1,512,768]{2,1,0:T(8,128)S(1)}, u32[]{:S(2)}) copy-start(f32[1,512,768]{2,1,0:T(8,128)S(1)} %get-tuple-element.709) | copy-start | bytes 4718596
  181.0 21.1 %copy-start.74 = (f32[512]{0:T(512)}, f32[512]{0:T(512)S(1)}, u32[]{:S(2)}) copy-start(f32[512]{0:T(512)S(1)} %broadcast_multiply_fusion.3) | copy-start | bytes 6148
  181.3 20.8 %copy-start.78 = (f32[512]{0:T(512)}, f32[512]{0:T(512)S(1)}, u32[]{:S(2)}) copy-start(f32[512]{0:T(512)S(1)} %fusion.137) | copy-start | bytes 6148
  183.9 14.4 %slice-start = ((s8[9437184]{0:T(1024)(128)(4,1)}), s8[4194304]{0:T(1024)(128)(4,1)S(1)}, s32[]{:S(2)}) async-start(s8[9437184]{0:T(1024)(128)(4,1)} %bitcast.436), calls=%async_computation.19 | async-start | bytes 8388608
  186.6 15.5 %copy-start.28 = (f32[512,3072]{1,0:T(8,128)}, f32[512,3072]{1,0:T(8,128)S(1)}, u32[]{:S(2)}) copy-start(f32[512,3072]{1,0:T(8,128)S(1)} %fusion.152) | copy-start | bytes 18874372
  186.6 11.8 %slice-start.1 = ((s8[9437184]{0:T(1024)(128)(4,1)}), s8[4194304]{0:T(1024)(128)(4,1)S(1)}, s32[]{:S(2)}) async-start(s8[9437184]{0:T(1024)(128)(4,1)} %bitcast.436), calls=%async_computation.20 | async-start | bytes 8388608
  186.6 11.8 %slice-start.2 = ((s8[9437184]{0:T(1024)(128)(4,1)}), s8[1048576]{0:T(1024)(128)(4,1)S(1)}, s32[]{:S(2)}) async-start(s8[9437184]{0:T(1024)(128)(4,1)} %bitcast.436), calls=%async_computation.21 | async-start | bytes 2097152
  198.4 3.6 copy-start.42
  202.0 8.6 copy-start.29
  202.1 8.6 copy-start.19
  215.8 13.3 %copy-start.21 = (f32[2048,3]{1,0:T(8,128)S(1)}, f32[2048,3]{1,0:T(8,128)}, u32[]{:S(2)}) copy-start(f32[2048,3]{1,0:T(8,128)} %get-tuple-element.285) | copy-start | bytes 73732
  230.5 5.9 copy-start.15
  253.1 5.6 copy-start.2
  276.5 5.6 copy-start.2
  301.3 5.6 copy-start.2
  326.2 5.6 copy-start.2
  335.7 4.2 copy-start.5
  367.9 28.5 %all-to-all-start.6 = ((bf16[4,2,49152]{2,1,0:T(2,128)(2,1)}), bf16[4,2,49152]{2,1,0:T(2,128)(2,1)}, u32[]{:S(2)}, u32[]{:S(2)}) async-start(bf16[4,2,49152]{2,1,0:T(2,128)(2,1)} %reshape.990), calls=%async_computation.6 | async-start | bytes 1572864 | tf_op jit(solution)/shard_map/all_to_all | solution.py:264
  392.4 8.5 copy-start.27
  396.4 33.0 %all-to-all-start.5 = ((bf16[4,2,49152]{2,1,0:T(2,128)(2,1)}), bf16[4,2,49152]{2,1,0:T(2,128)(2,1)}, u32[]{:S(2)}, u32[]{:S(2)}) async-start(bf16[4,2,49152]{2,1,0:T(2,128)(2,1)} %reshape.992), calls=%async_computation.5 | async-start | bytes 1572864 | tf_op jit(solution)/shard_map/all_to_all | solution.py:263
  400.6 105.5 %reduce-scatter.10.cloned.1.call-start = ((), (), s32[]{:S(2)}) async-start(), calls=%async_computation.15 | async-start | bytes 2654208 | tf_op jit(solution)/shard_map/reduce_scatter | solution.py:313
  429.3 20.0 %all-to-all-start.7 = ((bf16[4,2,49152]{2,1,0:T(2,128)(2,1)}), bf16[4,2,49152]{2,1,0:T(2,128)(2,1)S(1)}, u32[]{:S(2)}, u32[]{:S(2)}) async-start(bf16[4,2,49152]{2,1,0:T(2,128)(2,1)} %reshape.988), calls=%async_computation.7 | async-start | bytes 1572864 | tf_op jit(solution)/shard_map/all_to_all | solution.py:265
  433.5 86.1 %reduce-scatter.6.cloned.1.call-start = ((), (), s32[]{:S(2)}) async-start(), calls=%async_computation.13 | async-start | bytes 2654208 | tf_op jit(solution)/shard_map/reduce_scatter | solution.py:311
  464.9 3.2 copy-start.34
  473.9 3.8 copy-start.94
  477.7 3.6 copy-start.60
  477.7 3.7 copy-start.41
  481.3 117.1 %reduce-scatter.8.cloned.1.call-start = ((), (), s32[]{:S(2)}) async-start(), calls=%async_computation.14 | async-start | bytes 7962624 | tf_op jit(solution)/shard_map/reduce_scatter | solution.py:312
  486.3 212.1 %reduce-scatter.14.cloned.1.call-start = ((), (), s32[]{:S(2)}) async-start(), calls=%async_computation.17 | async-start | bytes 10616832 | tf_op jit(solution)/shard_map/reduce_scatter | solution.py:315
  497.9 300.6 %reduce-scatter.12.cloned.1.call-start = ((), (), s32[]{:S(2)}) async-start(), calls=%async_computation.16 | async-start | bytes 10616832 | tf_op jit(solution)/shard_map/reduce_scatter | solution.py:314
  506.0 292.5 %copy-start.95 = (u32[32]{0:T(128)S(1)}, u32[32]{0:T(128)}, u32[]{:S(2)}) copy-start(u32[32]{0:T(128)} %constant.187) | copy-start | bytes 388
  506.0 295.0 %copy-start.65 = (f32[4608]{0:T(1024)S(1)}, f32[4608]{0:T(1024)}, u32[]{:S(2)}) copy-start(f32[4608]{0:T(1024)} %get-tuple-element.747) | copy-start | bytes 55300
  506.0 295.0 %copy-start.86 = (f32[768]{0:T(1024)S(1)}, f32[768]{0:T(1024)}, u32[]{:S(2)}) copy-start(f32[768]{0:T(1024)} %get-tuple-element.700) | copy-start | bytes 9220
  506.0 295.0 %copy-start.89 = (f32[3072]{0:T(1024)S(1)}, f32[3072]{0:T(1024)}, u32[]{:S(2)}) copy-start(f32[3072]{0:T(1024)} %get-tuple-element.702) | copy-start | bytes 36868
  506.0 295.0 %copy-start.91 = (f32[768]{0:T(1024)S(1)}, f32[768]{0:T(1024)}, u32[]{:S(2)}) copy-start(f32[768]{0:T(1024)} %get-tuple-element.620) | copy-start | bytes 9220
  506.1 321.8 %copy-start.36 = (bf16[128,4608]{1,0:T(8,128)(2,1)S(1)}, bf16[128,4608]{1,0:T(8,128)(2,1)}, u32[]{:S(2)}) copy-start(bf16[128,4608]{1,0:T(8,128)(2,1)} %param.29) | copy-start | bytes 3538948
  506.1 321.8 %copy-start.61 = (f32[2,4608]{1,0:T(2,128)S(1)}, f32[2,4608]{1,0:T(2,128)}, u32[]{:S(2)}) copy-start(f32[2,4608]{1,0:T(2,128)} %copy-done.60) | copy-start | bytes 110596
  506.1 393.9 %all-reduce.14.cloned.1.call-start = ((), (), s32[]{:S(2)}) async-start(), calls=%async_computation.18 | async-start | bytes 7667712 | tf_op jit(solution)/shard_map/psum | solution.py:334
  900.0 4.0 copy-start.62
  900.0 4.8 copy-start.50
  901.8 4.0 copy-start.49
  904.0 2.8 copy-start.1
  (39 other events, 62.9 us)
Sparse Core Ops, SparseCore 0:
  404.4 38.1 reduce-scatter.9
  481.4 38.1 reduce-scatter.5
  521.9 76.3 reduce-scatter.7
  600.5 97.8 reduce-scatter.13
  700.5 97.8 reduce-scatter.11
  802.0 97.9 all-reduce.13
where the time goes:
time: 925 us; the launch traced here: 914 us
  waiting for transfers between devices  363 us (39%)
  matrix products  176 us (19%)
  local copies, waits for them, and re-layouts  160 us (17%)
  other arithmetic  108 us (12%)
  blocking collectives  61.7 us (7%)
  starting transfers between devices  26.5 us (3%)
  between operations  18.2 us (2%)
    reduce_scatter x1, waiting for transfers between devices, body(): lax.psum_scatter(sum_w_down, 'wide', scatter_dimension=0, tiled=True)  100 us
    reduce_scatter x1, waiting for transfers between devices, body(): lax.psum_scatter(sum_w_up, 'wide', scatter_dimension=0, tiled=True)  100 us
    reduce_scatter x1, waiting for transfers between devices, body(): lax.psum_scatter(sum_w_qkv, 'wide', scatter_dimension=0, tiled=True)  78.7 us
    psum x1, waiting for transfers between devices, body(): lax.psum((share_ada, share_qkv, share_out, share_up, share_down, piece_ad...  60.2 us
    unnamed x190, local copies, waits for them, and re-layouts  58.1 us
    unnamed x8, other arithmetic  53.8 us
    unnamed x1, blocking collectives  26.4 us
    dot_general x4, matrix products, step(): jnp.einsum('shqk,kshd->qshd', grad_scores, keys_doc, preferred_element_ty...  22.6 us
  transfers between devices with their start and end apart: 12, of which 8 were waited for; matrix products, arithmetic and copies ran while one was open for 15% of the time, Pallas kernels for 0%

commit v1 on v0

--- a/solution.py
+++ b/solution.py
@@ -199,13 +199,16 @@
     key_h = head_view(key_h)
     value_h = head_view(value_h)
     mixed_h, logsum = lax.map(attend_row, (query_h, key_h, value_h, docs_per_row))
-    mixed = lax.all_to_all(
-        mixed_h.reshape(count_rows, length, 1, group * head_dim),
-        "narrow",
-        split_axis=1,
-        concat_axis=2,
-        tiled=True,
-    )
+    shard = mixed_h.reshape(count_rows, length, 1, group * head_dim)
+    ways, here = (lax.axis_size("narrow"), lax.axis_index("narrow"))
+    width_2 = shard.shape[1] // ways
+    turned_2 = jnp.roll(shard, -here * width_2, axis=1)
+    got = [lax.slice_in_dim(turned_2, 0, width_2, axis=1)]
+    for far in range(1, ways):
+        sent = lax.slice_in_dim(turned_2, far * width_2, (far + 1) * width_2, axis=1)
+        got.append(lax.ppermute(sent, "narrow", [(d, (d + far) % ways) for d in range(ways)]))
+    line = jnp.concatenate(got[::-1], axis=2)
+    mixed = jnp.roll(line, (here + 1) * got[0].shape[2], axis=2)
     attended = mixed.reshape(count_rows * local, width)
     branch = jnp.dot(attended, w_out, preferred_element_type=jnp.float32).reshape(
         count_rows, local, width

time: 925 us -> 893 us (0.965)
  other arithmetic: 108 us -> 92.4 us
  local copies, waits for them, and re-layouts: 160 us -> 147 us
    unnamed x8 -> x5, other arithmetic: 53.8 us -> 40.2 us
    all_to_all x3 -> x0, local copies, waits for them, and re-layouts: 10.2 us -> none  [body(): lax.all_to_all(mixed_h.reshape(count_rows, length, 1, group * head_dim),...]
    unnamed x190 -> x193, local copies, waits for them, and re-layouts: 58.1 us -> 62.5 us
  transfers between devices with their start and end apart: 12 -> 14, of which waited for: 8 -> 9; matrix products, arithmetic and copies ran while one was open for 15% -> 16% of each run, Pallas kernels for 0% -> 0%
where the time goes in v1:
time: 893 us; the launch traced here: 882 us
  waiting for transfers between devices  361 us (40%)
  matrix products  175 us (20%)
  local copies, waits for them, and re-layouts  147 us (16%)
  other arithmetic  92.4 us (10%)
  blocking collectives  61.6 us (7%)
  starting transfers between devices  25.5 us (3%)
  between operations  18.3 us (2%)
    reduce_scatter x1, waiting for transfers between devices, body(): lax.psum_scatter(sum_w_down, 'wide', scatter_dimension=0, tiled=True)  100 us
    reduce_scatter x1, waiting for transfers between devices, body(): lax.psum_scatter(sum_w_up, 'wide', scatter_dimension=0, tiled=True)  100 us
    reduce_scatter x1, waiting for transfers between devices, body(): lax.psum_scatter(sum_w_qkv, 'wide', scatter_dimension=0, tiled=True)  78.8 us
    unnamed x193, local copies, waits for them, and re-layouts  62.5 us
    psum x1, waiting for transfers between devices, body(): lax.psum((share_ada, share_qkv, share_out, share_up, share_down, piece_ad...  59.6 us
    unnamed x5, other arithmetic  40.2 us
    unnamed x1, blocking collectives  26.4 us
    dot_general x4, matrix products, step(): jnp.einsum('shqk,kshd->qshd', grad_scores, keys_doc, preferred_element_ty...  22.6 us
  transfers between devices with their start and end apart: 14, of which 9 were waited for; matrix products, arithmetic and copies ran while one was open for 16% of the time, Pallas kernels for 0%

profile of v1, /device:TPU:0, one launch (start us, length us, event | category | flops | bytes accessed | tf_op | source)
XLA Modules:
  0.0 882.2 jit_solution(2121860441337367043)
XLA Ops:
  11.4 5.9 copy.302
  18.3 3.9 convolution_bitcast_fusion
  22.7 4.2 copy-done.40
  31.4 5.2 all-to-all-start.2
  42.8 4.6 all-to-all-done.2
  47.4 13.2 %all_to_all.87 = bf16[1,512,4,192]{1,3,0,2:T(8,128)(2,1)S(1)} all-to-all(bf16[1,512,4,192]{1,3,0,2:T(8,128)(2,1)S(1)} %get-tuple-element.723), channel_id=1, replica_groups=mesh['narrow'=4,'wide'=8] {'narrow'}, dimensions={2} | all-to-all | bytes 1572864 | tf_op jit(solution)/shard_map/all_to_all | solution.py:193
  60.6 4.0 all-to-all-start
  77.7 45.2 %conditional.2 = (bf16[2048,3,64]{2,1,0:T(4,128)(2,1)}, f32[2048,3]{1,0:T(8,128)}) conditional(s32[]{:T(128)} %convert_element_type.263, (bf16[2048,3,64]{0,2,1:T(8,128)(2,1)}, bf16[2048,3,64]{0,2,1:T(8,128)(2,1)S(1)}, bf16[2048,3,64]{0,2,1:T(8,128)(2,1)S(1)}) %tuple.47, (bf16[2048,3,64]{0,2,1:T(8,128)(2,1)}, bf16[2048,3,64]{0,2,1:T(8,128)(2,1)S(1)}, ...), branch_computations={%region_2.7_spmd, %region_7.12_spmd} | conditional | flops 833811456 | bytes 64065880 | solution.py:124
  82.1 36.1 %while.50 = (s32[]{:T(128)}, bf16[4,512,1,3,64]{1,4,3,2,0:T(8,128)(2,1)}, f32[4,1,3,512]{3,2,1,0:T(4,128)}, bf16[4,512,1,3,64]{1,4,3,2,0:T(8,128)(2,1)S(1)}, bf1...) while((s32[]{:T(128)}, bf16[4,512,1,3,64]{1,4,3,2,0:T(8,128)(2,1)}, ...), condition=%wide.region_11.11_spmd, body=%wide.region_8.10_spmd.sunk | while | flops 833714688 | bytes 39766112 | solution.py:66
  86.5 4.0 fusion.246
  95.6 4.0 fusion.246
  104.6 4.0 fusion.246
  113.6 4.0 fusion.246
  122.9 3.9 copy.312
  140.4 3.7 collective-permute-done.2
  148.0 3.8 fusion.148
  158.1 11.8 %convert_reduce_fusion = (f32[3072]{0:T(1024)}, bf16[512,3072]{1,0:T(8,128)(2,1)S(1)}) fusion(f32[512,3072]{1,0:T(8,128)S(1)} %fusion.154, f32[3072]{0:T(1024)S(1)} %copy-done.91, bf16[512,768]{1,0:T(8,128)(2,1)S(1)} %copy-done.55, bf16[3072,768]{1,0:T(8,128)(2,1)} %param.37), kind=kOutput, calls=%fused_computation.105 | convolution fusion | flops 2458383360 | bytes 14966784 | tf_op jit(solution)/shard_map/td,fd->tf/dot_general | solution.py:235
  173.6 8.5 fusion.147
  185.3 11.1 %all_to_all.88 = bf16[1,512,4,192]{1,3,0,2:T(8,128)(2,1)S(1)} all-to-all(bf16[1,512,4,192]{1,3,0,2:T(8,128)(2,1)S(1)} %bitcast.474), channel_id=1, replica_groups=mesh['narrow'=4,'wide'=8] {'narrow'}, dimensions={2} | all-to-all | bytes 1572864 | tf_op jit(solution)/shard_map/all_to_all | solution.py:250
  198.5 113.9 %conditional.3 = (bf16[2048,3,64]{2,1,0:T(4,128)(2,1)}, bf16[2048,3,64]{2,1,0:T(4,128)(2,1)}, bf16[2048,3,64]{2,1,0:T(4,128)(2,1)S(1)}) conditional(s32[]{:T(128)} %convert_element_type.263, (bf16[2048,3,64]{0,2,1:T(8,128)(2,1)}, f32[2048,3]{1,0:T(8,128)S(1)}, bf16[2048,3,64]{0,2,1:T(8,128)(2,1)}, bf16[2048,3,64]{0,2,1:T(8,128)(2,1)S(1)}, ...), branch_computations={%region_16.20_spmd, %region_20.24_spmd} | conditional | flops 2053174272 | bytes 155857408 | solution.py:131
  205.1 96.5 %while.53 = (s32[]{:T(128)}, f32[2048,1,3,64]{0,3,2,1:T(8,128)}, f32[2048,1,3,64]{0,3,2,1:T(8,128)}, bf16[4,512,1,3,64]{1,4,3,2,0:T(8,128)(2,1)}, bf16[4,512,1,3...) while((s32[]{:T(128)}, f32[2048,1,3,64]{0,3,2,1:T(8,128)}, ...), condition=%wide.region_23.23_spmd.clone, body=%wide.region_21.22_spmd.clone.sunk | while | flops 2053077504 | bytes 129415344 | solution.py:111
  207.0 3.7 fusion.231
  210.7 3.6 multiply_reduce_fusion.11
  214.4 4.7 multiply_convert_fusion.8
  219.1 5.6 fusion.232
  229.0 5.1 fusion.231
  234.2 3.6 multiply_reduce_fusion.11
  237.8 4.7 multiply_convert_fusion.8
  242.5 5.6 fusion.232
  248.1 3.9 fusion.230
  253.9 5.1 fusion.231
  259.0 3.6 multiply_reduce_fusion.11
  262.6 4.7 multiply_convert_fusion.8
  267.3 5.6 fusion.232
  273.0 3.9 fusion.230
  278.7 5.1 fusion.231
  287.5 4.7 multiply_convert_fusion.8
  292.2 5.6 fusion.232
  297.8 3.9 fusion.230
  301.7 4.2 copy.299
  315.2 3.8 copy.327
  319.5 12.7 %reduce.19 = bf16[2048,192]{1,0:T(8,128)(2,1)S(1)} reduce(bf16[2048,1,1,192]{3,2,1,0:T(2,128)(2,1)} %bitcast.446, bf16[]{:T(256)} %broadcast.563), dimensions={1,2}, to_apply=%bitcast.289.reduce_sub_computation | reduce | bytes 1572866
  334.6 4.2 all-to-all-start.5
  341.6 3.8 copy.323
  345.4 13.6 %reduce.18 = bf16[2048,192]{1,0:T(8,128)(2,1)} reduce(bf16[2048,1,1,192]{3,2,1,0:T(2,128)(2,1)} %bitcast.448, bf16[]{:T(256)} %broadcast.563), dimensions={1,2}, to_apply=%bitcast.291.reduce_sub_computation | reduce | bytes 1572866
  359.0 4.0 reshape.989
  363.0 4.2 all-to-all-start.4
  373.6 11.6 %reduce.17 = bf16[2048,192]{1,0:T(8,128)(2,1)S(1)} reduce(bf16[2048,1,1,192]{3,2,1,0:T(2,128)(2,1)S(1)} %bitcast.447, bf16[]{:T(256)} %broadcast.563), dimensions={1,2}, to_apply=%bitcast.287.reduce_sub_computation | reduce | bytes 1572866
  396.0 4.1 all-to-all-start.6
  400.1 4.2 reshape.990
  404.3 4.5 copy.324
  418.6 4.7 copy.332
  441.6 3.8 fusion.153
  446.0 3.7 fusion.139
  450.8 5.0 fusion.121
  456.9 10.4 %fusion.143 = f32[3072,768]{1,0:T(8,128)} fusion(bf16[512,768]{1,0:T(8,128)(2,1)S(1)} %copy-done.56, f32[512,3072]{1,0:T(8,128)} %copy-done.28, f32[3072]{0:T(1024)S(1)} %copy-done.92), kind=kOutput, calls=%fused_computation.236 | convolution fusion | flops 2431647744 | bytes 16527360 | tf_op jit(solution)/shard_map/tf,td->fd/dot_general | solution.py:234
  468.4 7.0 fusion.156
  475.5 12.3 %reduce-scatter.6.cloned.1.call-done = f32[576,128]{1,0:T(8,128)} async-done(((f32[4608,128]{1,0:T(8,128)}), f32[576,128]{1,0:T(8,128)}) %reduce-scatter.6.cloned.1.call-update) | async-done | bytes 294928 | tf_op jit(solution)/shard_map/reduce_scatter | solution.py:314
  487.8 78.8 %reduce-scatter.8.cloned.1.call-done = f32[96,2304]{1,0:T(8,128)} async-done(((f32[768,2304]{1,0:T(8,128)}), f32[96,2304]{1,0:T(8,128)}) %reduce-scatter.8.cloned.1.call-update) | async-done | bytes 884752 | tf_op jit(solution)/shard_map/reduce_scatter | solution.py:315
  566.6 100.1 %reduce-scatter.14.cloned.1.call-done = f32[384,768]{1,0:T(8,128)} async-done(((f32[3072,768]{1,0:T(8,128)}), f32[384,768]{1,0:T(8,128)}) %reduce-scatter.14.cloned.1.call-update) | async-done | bytes 1179664 | tf_op jit(solution)/shard_map/reduce_scatter | solution.py:318
  666.7 100.1 %reduce-scatter.12.cloned.1.call-done = f32[96,3072]{1,0:T(8,128)} async-done(((f32[768,3072]{1,0:T(8,128)}), f32[96,3072]{1,0:T(8,128)}) %reduce-scatter.12.cloned.1.call-update) | async-done | bytes 1179664 | tf_op jit(solution)/shard_map/reduce_scatter | solution.py:317
  769.9 26.4 %all-reduce.9 = (f32[4608]{0:T(1024)S(1)}, f32[768]{0:T(1024)S(1)}, f32[768]{0:T(1024)S(1)}, f32[3072]{0:T(1024)S(1)}, f32[768]{0:T(1024)S(1)}) all-reduce(f32[4608]{0:T(1024)S(1)} %copy-done.69, f32[768]{0:T(1024)S(1)} %get-tuple-element.622, f32[768]{0:T(1024)S(1)} %copy-done.96, ...), channel_id=3, replica_groups=mesh['narrow'=4,'wide'=8] {'wide'}, use_global_device_ids=true, to_apply=%region_30.31.clone | all-reduce | flops 9984 | bytes 79872
  797.7 10.9 %all-reduce.10 = (f32[1,2,128]{2,1,0:T(2,128)}, f32[576]{0:T(1024)}, f32[96]{0:T(128)}, f32[96]{0:T(128)}, f32[384]{0:T(512)}, /*index=5*/f32[96]{0:T(128)}) all-reduce(f32[1,2,128]{2,1,0:T(2,128)S(1)} %convolution_bitcast_fusion.2, f32[576]{0:T(1024)S(1)} %dynamic-slice.2, ...), channel_id=1, replica_groups=mesh['narrow'=4,'wide'=8] {'narrow'}, use_global_device_ids=true, to_apply=%region_26.27 | all-reduce | flops 1504 | bytes 12032 | tf_op jit(solution)/shard_map/psum | solution.py:337
  808.6 59.6 %all-reduce.14.cloned.1.call-done = (f32[128,576]{0,1:T(8,128)}, f32[96,2304]{1,0:T(8,128)}, f32[96,768]{1,0:T(8,128)}, f32[96,3072]{1,0:T(8,128)}, f32[384,768]{1,0:T(8,128)}) async-done(((f32[128,576]{0,1:T(8,128)}, f32[96,2304]{1,0:T(8,128)}, f32[96,768]{1,0:T(8,128)}, f32[96,3072]{1,0:T(8,128)}, f32[384,768]{1,0:T(8,128)}), (f32[128,576]{0,1:T(8,128)}, f32[96,2304]{1,0:T(8,128)}, f32[96,768]{1,0:T(8,128)}, ...) | async-done | bytes 3833872 | tf_op jit(solution)/shard_map/psum | solution.py:337
  (340 shorter events, 183.0 us)
Async XLA Ops:
  7.2 140.8 %copy-start = (bf16[768,768]{1,0:T(8,128)(2,1)S(1)}, bf16[768,768]{1,0:T(8,128)(2,1)}, u32[]{:S(2)}) copy-start(bf16[768,768]{1,0:T(8,128)(2,1)} %param.33) | copy-start | bytes 3538948
  7.2 3.6 copy-start.97
  7.2 4.2 copy-start.94
  9.3 12.9 %copy-start.72 = (f32[512]{0:T(512)}, f32[512]{0:T(512)S(1)}, u32[]{:S(2)}) copy-start(f32[512]{0:T(512)S(1)} %broadcast_multiply_fusion.4) | copy-start | bytes 6148
  10.8 11.4 %copy-start.74 = (f32[512]{0:T(512)}, f32[512]{0:T(512)S(1)}, u32[]{:S(2)}) copy-start(f32[512]{0:T(512)S(1)} %fusion.137) | copy-start | bytes 6148
  11.4 10.8 %copy-start.67 = (f32[768]{0:T(1024)}, f32[768]{0:T(1024)S(1)}, u32[]{:S(2)}) copy-start(f32[768]{0:T(1024)S(1)} %convert_element_type.264) | copy-start | bytes 9220
  11.4 5.9 copy-start.35
  11.4 5.9 copy-start.99
  18.3 3.9 copy-start.8
  22.2 6.7 copy-start.6
  22.2 4.7 copy-start.40
  22.7 6.2 copy-start.42
  28.9 2.4 copy-start.41
  31.4 16.0 %all-to-all-start.2 = ((bf16[1,512,4,192]{1,3,0,2:T(8,128)(2,1)}), bf16[1,512,4,192]{1,3,0,2:T(8,128)(2,1)S(1)}, u32[]{:S(2)}, u32[]{:S(2)}) async-start(bf16[1,512,4,192]{1,3,0,2:T(8,128)(2,1)} %bitcast.65), calls=%async_computation.2 | async-start | bytes 1572864 | tf_op jit(solution)/shard_map/all_to_all | solution.py:194
  60.6 12.9 %all-to-all-start = ((bf16[1,512,4,192]{1,3,0,2:T(8,128)(2,1)}), bf16[1,512,4,192]{1,3,0,2:T(8,128)(2,1)S(1)}, u32[]{:S(2)}, u32[]{:S(2)}) async-start(bf16[1,512,4,192]{1,3,0,2:T(8,128)(2,1)} %get-tuple-element.724), calls=%async_computation | async-start | bytes 1572864 | tf_op jit(solution)/shard_map/all_to_all | solution.py:192
  126.8 6.1 copy-start.19
  130.0 9.4 %collective-permute-start.1 = (bf16[1,512,1,192]{1,3,2,0:T(8,128)(2,1)}, bf16[1,512,1,192]{1,3,2,0:T(8,128)(2,1)}, u32[]{:S(2)}, u32[]{:S(2)}) collective-permute-start(bf16[1,512,1,192]{1,3,2,0:T(8,128)(2,1)} %get-tuple-element.737), channel_id=1, source_target_pairs={{0,16},{8,24},{16,0},{24,8},{1,17},{9,25},{17,1},{25,9},{2,18},{10... | collective-permute-start | bytes 589832 | tf_op jit(solution)/shard_map/ppermute | solution.py:209
  131.5 4.4 copy-start.98
  131.5 5.1 copy-start.95
  131.5 7.0 collective-permute-start
  135.9 37.6 %copy-start.76 = (f32[768]{0:T(1024)}, f32[768]{0:T(1024)S(1)}, u32[]{:S(2)}) copy-start(f32[768]{0:T(1024)S(1)} %convert_element_type.270) | copy-start | bytes 9220
  136.6 36.9 %copy-start.88 = (f32[768]{0:T(1024)}, f32[768]{0:T(1024)S(1)}, u32[]{:S(2)}) copy-start(f32[768]{0:T(1024)S(1)} %convert_element_type.274) | copy-start | bytes 9220
  137.2 6.8 collective-permute-start.2
  145.0 3.0 copy-start.9
  147.9 5.2 copy-start.7
  148.0 3.8 copy-start.26
  151.8 21.7 %copy-start.13 = (f32[1,512,768]{2,1,0:T(8,128)}, f32[1,512,768]{2,1,0:T(8,128)S(1)}, u32[]{:S(2)}) copy-start(f32[1,512,768]{2,1,0:T(8,128)S(1)} %get-tuple-element.709) | copy-start | bytes 4718596
  151.9 21.7 %copy-start.78 = (f32[512]{0:T(512)}, f32[512]{0:T(512)S(1)}, u32[]{:S(2)}) copy-start(f32[512]{0:T(512)S(1)} %broadcast_multiply_fusion.3) | copy-start | bytes 6148
  153.1 20.5 %copy-start.82 = (f32[512]{0:T(512)}, f32[512]{0:T(512)S(1)}, u32[]{:S(2)}) copy-start(f32[512]{0:T(512)S(1)} %fusion.138) | copy-start | bytes 6148
  153.1 2.3 copy-start.37
  155.5 2.6 copy-start.22
  155.5 2.6 copy-start.55
  155.5 2.6 copy-start.91
  158.1 15.5 %copy-start.28 = (f32[512,3072]{1,0:T(8,128)}, f32[512,3072]{1,0:T(8,128)S(1)}, u32[]{:S(2)}) copy-start(f32[512,3072]{1,0:T(8,128)S(1)} %fusion.154) | copy-start | bytes 18874372
  169.9 3.6 copy-start.44
  173.5 8.6 copy-start.29
  199.6 2.7 copy-start.16
  219.1 5.6 copy-start.2
  242.5 5.6 copy-start.2
  267.3 5.6 copy-start.2
  292.2 5.6 copy-start.2
  301.7 4.2 copy-start.5
  334.6 28.5 %all-to-all-start.5 = ((bf16[4,2,49152]{2,1,0:T(2,128)(2,1)}), bf16[4,2,49152]{2,1,0:T(2,128)(2,1)}, u32[]{:S(2)}, u32[]{:S(2)}) async-start(bf16[4,2,49152]{2,1,0:T(2,128)(2,1)} %reshape.987), calls=%async_computation.5 | async-start | bytes 1572864 | tf_op jit(solution)/shard_map/all_to_all | solution.py:267
  359.0 8.4 copy-start.27
  363.0 32.9 %all-to-all-start.4 = ((bf16[4,2,49152]{2,1,0:T(2,128)(2,1)}), bf16[4,2,49152]{2,1,0:T(2,128)(2,1)}, u32[]{:S(2)}, u32[]{:S(2)}) async-start(bf16[4,2,49152]{2,1,0:T(2,128)(2,1)} %reshape.989), calls=%async_computation.4 | async-start | bytes 1572864 | tf_op jit(solution)/shard_map/all_to_all | solution.py:266
  367.2 108.2 %reduce-scatter.10.cloned.1.call-start = ((), (), s32[]{:S(2)}) async-start(), calls=%async_computation.14 | async-start | bytes 2654208 | tf_op jit(solution)/shard_map/reduce_scatter | solution.py:316
  396.0 20.0 %all-to-all-start.6 = ((bf16[4,2,49152]{2,1,0:T(2,128)(2,1)}), bf16[4,2,49152]{2,1,0:T(2,128)(2,1)S(1)}, u32[]{:S(2)}, u32[]{:S(2)}) async-start(bf16[4,2,49152]{2,1,0:T(2,128)(2,1)} %reshape.985), calls=%async_computation.6 | async-start | bytes 1572864 | tf_op jit(solution)/shard_map/all_to_all | solution.py:268
  400.1 87.7 %reduce-scatter.6.cloned.1.call-start = ((), (), s32[]{:S(2)}) async-start(), calls=%async_computation.12 | async-start | bytes 2654208 | tf_op jit(solution)/shard_map/reduce_scatter | solution.py:314
  423.4 2.2 copy-start.50
  432.2 2.4 copy-start.85
  432.2 3.2 copy-start.34
  441.6 4.4 copy-start.100
  449.7 116.9 %reduce-scatter.8.cloned.1.call-start = ((), (), s32[]{:S(2)}) async-start(), calls=%async_computation.13 | async-start | bytes 7962624 | tf_op jit(solution)/shard_map/reduce_scatter | solution.py:315
  455.8 210.9 %reduce-scatter.14.cloned.1.call-start = ((), (), s32[]{:S(2)}) async-start(), calls=%async_computation.16 | async-start | bytes 10616832 | tf_op jit(solution)/shard_map/reduce_scatter | solution.py:318
  467.3 299.4 %reduce-scatter.12.cloned.1.call-start = ((), (), s32[]{:S(2)}) async-start(), calls=%async_computation.15 | async-start | bytes 10616832 | tf_op jit(solution)/shard_map/reduce_scatter | solution.py:317
  475.4 392.8 %all-reduce.14.cloned.1.call-start = ((), (), s32[]{:S(2)}) async-start(), calls=%async_computation.17 | async-start | bytes 7667712 | tf_op jit(solution)/shard_map/psum | solution.py:337
  766.7 3.2 copy-start.69
  766.7 3.2 copy-start.90
  766.7 3.2 copy-start.93
  766.7 3.2 copy-start.96
  766.7 30.0 %copy-start.36 = (bf16[128,4608]{1,0:T(8,128)(2,1)S(1)}, bf16[128,4608]{1,0:T(8,128)(2,1)}, u32[]{:S(2)}) copy-start(bf16[128,4608]{1,0:T(8,128)(2,1)} %param.29) | copy-start | bytes 3538948
  766.7 30.0 %copy-start.65 = (f32[2,4608]{1,0:T(2,128)S(1)}, f32[2,4608]{1,0:T(2,128)}, u32[]{:S(2)}) copy-start(f32[2,4608]{1,0:T(2,128)} %copy-done.64) | copy-start | bytes 110596
  868.2 3.9 copy-start.66
  868.2 4.7 copy-start.52
  (41 other events, 57.2 us)
Sparse Core Ops, SparseCore 0:
  371.0 37.9 reduce-scatter.9
  449.8 37.9 reduce-scatter.5
  490.1 76.3 reduce-scatter.7
  568.7 97.8 reduce-scatter.13
  668.8 97.8 reduce-scatter.11
  770.3 97.9 all-reduce.13
